TPU v7x, 32 devices: a whole 2x2x4 slice. The times are simulated.
32 devices in a mesh: sub: 16 (over z, y, core), col: 2 (over x).
Axes of the slice: x: 2, y: 2, z: 4, core: 2. Of those that a mesh axis runs over, the one named last changes fastest.
Arguments:
- right_sides: float32 [64, 20480], P(None, ('sub', 'col')), may hold values from -6 to 6
- operator: float32 [16, 1536, 1280], P('sub', None, 'col'), may hold values from -0.15625 to 0.15625
- local_inverse: float32 [16, 1536, 1280], P('sub', None, 'col'), may hold values from -0.15625 to 0.15625
- coarse_basis: float32 [16, 1536, 64], P('sub'), may hold values from -0.15625 to 0.15625
- coarse_inverse: float32 [1024, 1024], P('sub', 'col'), may hold values from -0.5 to 0.5
- send_index: int32 [16, 2, 4, 32], P('sub', 'col'), may hold values from 0 to 639
- halo_count: int32 [16, 2, 4], P('sub', 'col'), may hold values from 1 to 32, as said below
Outputs:
- solution: float32 [64, 20480], P(None, ('sub', 'col'))
- residual: float32 [64, 20480], P(None, ('sub', 'col'))
Inputs may be any that keep to these rules, and one draw needn't show every extreme that they name: `halo_count`: on every device of every draw at least one of its 4 counts equals 32.
All inputs are finite; a program needn't handle non-finite values.
Results may differ from a plain program's by a relative error of at most 0.000078.
Values sent between devices are 32-bit elements; how exact they have to be, the bound alone decides.
A program may use at most 64 MiB of HBM per device.

v0:
```python
import jax
import jax.numpy as jnp
from jax import lax
from jax.sharding import PartitionSpec as P

HIGH = lax.Precision.HIGHEST


def passed_along(block, axis, distance):
    devices = range(lax.axis_size(axis))
    route = [(i - distance, i) for i in devices if i - distance in devices]
    return lax.ppermute(block, axis, route)


def body(
    right_sides, operator, local_inverse, coarse_basis, coarse_inverse, send_index, halo_count
):
    own_width = right_sides.shape[1]
    rhs_width = right_sides.shape[0]
    halo_slots = send_index.shape[3]
    stride = lax.axis_size("sub") // 4
    offsets = (1, -1, stride, -stride)
    send_rows = send_index[0, 0]
    counts = halo_count[0, 0]
    live_slots = (jnp.arange(halo_slots, dtype=jnp.int32)[None, :] < counts[:, None]).astype(
        jnp.float32
    )
    operator_rows = operator[0]
    inverse_rows = local_inverse[0]
    basis_rows = coarse_basis[0]
    mode_count = basis_rows.shape[1]
    block_len = basis_rows.shape[0] // lax.axis_size("col")
    column_index = lax.axis_index("col")
    quarter = coarse_inverse.shape[1] // lax.axis_size("sub")

    def extend_apply(field, matrices):
        pieces = [field]
        for number in range(len(offsets)):
            packed = jnp.take(field, send_rows[number], axis=1) * live_slots[number][None, :]
            pieces.append(passed_along(packed, "sub", offsets[number]))
        own_and_halo = jnp.concatenate(pieces, axis=1)
        segment = lax.all_gather(own_and_halo, "col", axis=1, tiled=True)
        return tuple([jnp.dot(segment, matrix, precision=HIGH) for matrix in matrices])

    def precondition(field):
        local_part, coeff_rows = extend_apply(field, (inverse_rows, basis_rows))
        mode_coeffs = coeff_rows.T
        segment = lax.all_gather(
            mode_coeffs.reshape(1, mode_count * rhs_width), "sub", axis=0, tiled=True
        )
        held = segment.shape[0]
        blocks = segment.reshape(held, mode_count, rhs_width)
        kept_rows = lax.dynamic_slice_in_dim(blocks, column_index * quarter, quarter, 1).reshape(
            held * quarter, rhs_width
        )
        partial_sum = jnp.dot(coarse_inverse, kept_rows, precision=HIGH)
        coarse_vals = lax.psum(partial_sum, "col")
        own_basis = lax.dynamic_slice_in_dim(basis_rows, column_index * block_len, own_width, 0)
        coarse_part = lax.dot_general(
            coarse_vals, own_basis, (((0,), (1,)), ((), ())), precision=HIGH
        )
        return local_part + coarse_part

    first_pass = precondition(right_sides)
    applied_parts = extend_apply(first_pass, (operator_rows,))
    residual = right_sides - applied_parts[0]
    solution = first_pass + precondition(residual)
    return (solution, residual)


def solution(mesh):
    placed = (
        P(None, ("sub", "col")),
        P("sub", None, "col"),
        P("sub", None, "col"),
        P("sub", None, None),
        P("sub", "col"),
        P("sub", "col", None, None),
        P("sub", "col", None),
    )
    return jax.shard_map(
        body,
        mesh=mesh,
        in_specs=placed,
        out_specs=(P(None, ("sub", "col")), P(None, ("sub", "col"))),
        check_vma=False,
    )
```

profile of v0, /device:TPU:0, one launch (start us, length us, event | category | flops | bytes accessed | tf_op | source)
XLA Modules:
  0.0 146.8 jit_solution(18176462783339888928)
XLA Ops:
  4.1 1.3 collective-permute-start.1
  6.0 3.0 %collective-permute-start = (f32[64,32]{1,0:T(8,128)S(1)}, f32[64,32]{1,0:T(8,128)S(1)}, u32[]{:S(2)}, u32[]{:S(2)}) collective-permute-start(f32[64,32]{1,0:T(8,128)S(1)} %bitcast_multiply_fusion.11), channel_id=1, source_target_pairs={{0,2},{2,4},{4,6},{6,8},{8,10},{10,12},{12,14},{14,16},{16,18},{18... | collective-permute-start | bytes 24584 | tf_op jit(solution)/shard_map/ppermute | solution.py:12
  9.8 5.3 %collective-permute-start.2 = (f32[64,32]{1,0:T(8,128)S(1)}, f32[64,32]{1,0:T(8,128)S(1)}, u32[]{:S(2)}, u32[]{:S(2)}) collective-permute-start(f32[64,32]{1,0:T(8,128)S(1)} %bitcast_multiply_fusion.9), channel_id=1, source_target_pairs={{0,8},{2,10},{4,12},{6,14},{8,16},{10,18},{12,20},{14,22},{16,24},... | collective-permute-start | bytes 24584 | tf_op jit(solution)/shard_map/ppermute | solution.py:12
  15.7 1.3 collective-permute-start.3
  17.1 4.5 %collective-permute-done.3 = f32[64,32]{1,0:T(8,128)S(1)} collective-permute-done((f32[64,32]{1,0:T(8,128)S(1)}, f32[64,32]{1,0:T(8,128)S(1)}, u32[]{:S(2)}, u32[]{:S(2)}) %collective-permute-start.3) | collective-permute-done | bytes 8224 | tf_op jit(solution)/shard_map/ppermute | solution.py:12
  22.6 6.8 %all_gather.15 = f32[64,1536]{1,0:T(8,128)S(1)} all-gather(f32[64,768]{1,0:T(8,128)S(1)} %concatenate.9), channel_id=1, replica_groups=mesh['sub'=16,'col'=2] {'col'}, dimensions={1}, use_global_device_ids=true | all-gather | bytes 589824 | tf_op jit(solution)/shard_map/all_gather | solution.py:42
  30.0 20.4 %all-gather = f32[16,1,4096]{2,1,0:T(1,128)S(1)} all-gather(f32[1,1,4096]{2,1,0:T(1,128)S(1)} %reshape.151), channel_id=1, replica_groups=mesh['sub'=16,'col'=2] {'sub'}, dimensions={0}, use_global_device_ids=true | all-gather | bytes 278528 | tf_op jit(solution)/shard_map/all_gather | solution.py:48
  51.9 8.3 %psum.14 = f32[64,64]{0,1:T(8,128)S(1)} all-reduce(f32[64,64]{0,1:T(8,128)S(1)} %convolution_bitcast_fusion.3), channel_id=1, replica_groups=mesh['sub'=16,'col'=2] {'col'}, use_global_device_ids=true, to_apply=%region_0.0 | all-reduce | flops 4096 | bytes 32768 | tf_op jit(solution)/shard_map/psum | solution.py:57
  60.5 4.6 %fusion.6 = f32[64,640]{1,0:T(8,128)S(1)} fusion(f32[64,640]{1,0:T(8,128)S(1)} %fusion.22, f32[64,1536]{1,0:T(8,128)S(1)} %all_gather.15, f32[1,1536,640]{2,1,0:T(8,128)} %param.11), kind=kOutput, calls=%fused_computation.18 | convolution fusion | flops 755015680 | bytes 4653056 | tf_op jit(solution)/shard_map/dot_general | solution.py:43
  68.0 1.3 collective-permute-start.5
  69.3 3.0 %collective-permute-start.4 = (f32[64,32]{1,0:T(8,128)S(1)}, f32[64,32]{1,0:T(8,128)S(1)}, u32[]{:S(2)}, u32[]{:S(2)}) collective-permute-start(f32[64,32]{1,0:T(8,128)S(1)} %bitcast_multiply_fusion.7), channel_id=1, source_target_pairs={{0,2},{2,4},{4,6},{6,8},{8,10},{10,12},{12,14},{14,16},{16,18},{18... | collective-permute-start | bytes 24584 | tf_op jit(solution)/shard_map/ppermute | solution.py:12
  72.4 1.3 collective-permute-start.6
  73.7 1.3 collective-permute-start.7
  75.2 4.2 %collective-permute-done.7 = f32[64,32]{1,0:T(8,128)S(1)} collective-permute-done((f32[64,32]{1,0:T(8,128)S(1)}, f32[64,32]{1,0:T(8,128)S(1)}, u32[]{:S(2)}, u32[]{:S(2)}) %collective-permute-start.7) | collective-permute-done | bytes 8224 | tf_op jit(solution)/shard_map/ppermute | solution.py:12
  79.6 6.3 %all_gather.17 = f32[64,1536]{1,0:T(8,128)S(1)} all-gather(f32[64,768]{1,0:T(8,128)S(1)} %concatenate.10), channel_id=1, replica_groups=mesh['sub'=16,'col'=2] {'col'}, dimensions={1}, use_global_device_ids=true | all-gather | bytes 589824 | tf_op jit(solution)/shard_map/all_gather | solution.py:42
  85.9 4.6 %fusion.15 = f32[64,640]{1,0:T(8,128)S(1)} fusion(f32[64,640]{1,0:T(8,128)S(1)} %copy-done.1, f32[64,1536]{1,0:T(8,128)S(1)} %all_gather.17, f32[1,1536,640]{2,1,0:T(8,128)} %param.10), kind=kOutput, calls=%fused_computation.21 | convolution fusion | flops 755015680 | bytes 4653056 | tf_op jit(solution)/shard_map/dot_general | solution.py:43
  93.4 1.3 collective-permute-start.11
  94.7 4.5 %collective-permute-start.10 = (f32[64,32]{1,0:T(8,128)S(1)}, f32[64,32]{1,0:T(8,128)S(1)}, u32[]{:S(2)}, u32[]{:S(2)}) collective-permute-start(f32[64,32]{1,0:T(8,128)S(1)} %bitcast_multiply_fusion.1), channel_id=1, source_target_pairs={{0,8},{2,10},{4,12},{6,14},{8,16},{10,18},{12,20},{14,22},{16,24},... | collective-permute-start | bytes 24584 | tf_op jit(solution)/shard_map/ppermute | solution.py:12
  99.3 1.3 collective-permute-start.9
  100.6 3.0 %collective-permute-start.8 = (f32[64,32]{1,0:T(8,128)S(1)}, f32[64,32]{1,0:T(8,128)S(1)}, u32[]{:S(2)}, u32[]{:S(2)}) collective-permute-start(f32[64,32]{1,0:T(8,128)S(1)} %bitcast_multiply_fusion.3), channel_id=1, source_target_pairs={{0,2},{2,4},{4,6},{6,8},{8,10},{10,12},{12,14},{14,16},{16,18},{18... | collective-permute-start | bytes 24584 | tf_op jit(solution)/shard_map/ppermute | solution.py:12
  104.5 8.1 %all_gather.18 = f32[64,1536]{1,0:T(8,128)S(1)} all-gather(f32[64,768]{1,0:T(8,128)S(1)} %concatenate.11), channel_id=1, replica_groups=mesh['sub'=16,'col'=2] {'col'}, dimensions={1}, use_global_device_ids=true | all-gather | bytes 589824 | tf_op jit(solution)/shard_map/all_gather | solution.py:42
  113.3 19.0 %all-gather.1 = f32[16,1,4096]{2,1,0:T(1,128)S(1)} all-gather(f32[1,1,4096]{2,1,0:T(1,128)S(1)} %reshape.153), channel_id=1, replica_groups=mesh['sub'=16,'col'=2] {'sub'}, dimensions={0}, use_global_device_ids=true | all-gather | bytes 278528 | tf_op jit(solution)/shard_map/all_gather | solution.py:48
  133.8 7.4 %psum.15 = f32[64,64]{0,1:T(8,128)S(1)} all-reduce(f32[64,64]{0,1:T(8,128)S(1)} %convolution_bitcast_fusion.2), channel_id=1, replica_groups=mesh['sub'=16,'col'=2] {'col'}, use_global_device_ids=true, to_apply=%region_1.3 | all-reduce | flops 4096 | bytes 32768 | tf_op jit(solution)/shard_map/psum | solution.py:57
  141.5 5.3 %fusion.12 = f32[64,640]{1,0:T(8,128)} fusion(f32[64,640]{1,0:T(8,128)S(1)} %fusion.6, f32[64,640]{1,0:T(8,128)S(1)} %fusion.20, f32[64,1536]{1,0:T(8,128)S(1)} %all_gather.18, f32[1,1536,640]{2,1,0:T(8,128)} %param.11), kind=kOutput, calls=%fused_computation.20 | convolution fusion | flops 755056640 | bytes 4816896 | tf_op jit(solution)/shard_map/dot_general | solution.py:43
  (83 shorter events, 18.1 us)
Async XLA Ops:
  0.6 28.8 %copy-start = (f32[1,1536,64]{1,2,0:T(8,128)S(1)}, f32[1,1536,64]{1,2,0:T(8,128)}, u32[]{:S(2)}) copy-start(f32[1,1536,64]{1,2,0:T(8,128)} %param.12) | copy-start | bytes 1179652
  0.6 50.6 %copy-start.3 = (f32[64,512]{1,0:T(8,128)S(1)}, f32[64,512]{1,0:T(8,128)}, u32[]{:S(2)}) copy-start(f32[64,512]{1,0:T(8,128)} %param.13) | copy-start | bytes 393220
  4.1 13.0 %collective-permute-start.1 = (f32[64,32]{1,0:T(8,128)S(1)}, f32[64,32]{1,0:T(8,128)S(1)}, u32[]{:S(2)}, u32[]{:S(2)}) collective-permute-start(f32[64,32]{1,0:T(8,128)S(1)} %bitcast_multiply_fusion.10), channel_id=1, source_target_pairs={{2,0},{4,2},{6,4},{8,6},{10,8},{12,10},{14,12},{16,14},{18,16},{20... | collective-permute-start | bytes 24584 | tf_op jit(solution)/shard_map/ppermute | solution.py:12
  6.0 11.0 %collective-permute-start = (f32[64,32]{1,0:T(8,128)S(1)}, f32[64,32]{1,0:T(8,128)S(1)}, u32[]{:S(2)}, u32[]{:S(2)}) collective-permute-start(f32[64,32]{1,0:T(8,128)S(1)} %bitcast_multiply_fusion.11), channel_id=1, source_target_pairs={{0,2},{2,4},{4,6},{6,8},{8,10},{10,12},{12,14},{14,16},{16,18},{18... | collective-permute-start | bytes 24584 | tf_op jit(solution)/shard_map/ppermute | solution.py:12
  9.8 7.3 %collective-permute-start.2 = (f32[64,32]{1,0:T(8,128)S(1)}, f32[64,32]{1,0:T(8,128)S(1)}, u32[]{:S(2)}, u32[]{:S(2)}) collective-permute-start(f32[64,32]{1,0:T(8,128)S(1)} %bitcast_multiply_fusion.9), channel_id=1, source_target_pairs={{0,8},{2,10},{4,12},{6,14},{8,16},{10,18},{12,20},{14,22},{16,24},... | collective-permute-start | bytes 24584 | tf_op jit(solution)/shard_map/ppermute | solution.py:12
  15.7 5.8 %collective-permute-start.3 = (f32[64,32]{1,0:T(8,128)S(1)}, f32[64,32]{1,0:T(8,128)S(1)}, u32[]{:S(2)}, u32[]{:S(2)}) collective-permute-start(f32[64,32]{1,0:T(8,128)S(1)} %bitcast_multiply_fusion.8), channel_id=1, source_target_pairs={{8,0},{10,2},{12,4},{14,6},{16,8},{18,10},{20,12},{22,14},{24,16},... | collective-permute-start | bytes 24584 | tf_op jit(solution)/shard_map/ppermute | solution.py:12
  60.5 25.4 %copy-start.1 = (f32[64,640]{1,0:T(8,128)S(1)}, f32[64,640]{1,0:T(8,128)}, u32[]{:S(2)}) copy-start(f32[64,640]{1,0:T(8,128)} %param.9) | copy-start | bytes 491524
  68.0 6.9 %collective-permute-start.5 = (f32[64,32]{1,0:T(8,128)S(1)}, f32[64,32]{1,0:T(8,128)S(1)}, u32[]{:S(2)}, u32[]{:S(2)}) collective-permute-start(f32[64,32]{1,0:T(8,128)S(1)} %bitcast_multiply_fusion.6), channel_id=1, source_target_pairs={{2,0},{4,2},{6,4},{8,6},{10,8},{12,10},{14,12},{16,14},{18,16},{20... | collective-permute-start | bytes 24584 | tf_op jit(solution)/shard_map/ppermute | solution.py:12
  69.3 5.7 %collective-permute-start.4 = (f32[64,32]{1,0:T(8,128)S(1)}, f32[64,32]{1,0:T(8,128)S(1)}, u32[]{:S(2)}, u32[]{:S(2)}) collective-permute-start(f32[64,32]{1,0:T(8,128)S(1)} %bitcast_multiply_fusion.7), channel_id=1, source_target_pairs={{0,2},{2,4},{4,6},{6,8},{8,10},{10,12},{12,14},{14,16},{16,18},{18... | collective-permute-start | bytes 24584 | tf_op jit(solution)/shard_map/ppermute | solution.py:12
  72.4 2.9 %collective-permute-start.6 = (f32[64,32]{1,0:T(8,128)S(1)}, f32[64,32]{1,0:T(8,128)S(1)}, u32[]{:S(2)}, u32[]{:S(2)}) collective-permute-start(f32[64,32]{1,0:T(8,128)S(1)} %bitcast_multiply_fusion.5), channel_id=1, source_target_pairs={{0,8},{2,10},{4,12},{6,14},{8,16},{10,18},{12,20},{14,22},{16,24},... | collective-permute-start | bytes 24584 | tf_op jit(solution)/shard_map/ppermute | solution.py:12
  73.7 5.8 %collective-permute-start.7 = (f32[64,32]{1,0:T(8,128)S(1)}, f32[64,32]{1,0:T(8,128)S(1)}, u32[]{:S(2)}, u32[]{:S(2)}) collective-permute-start(f32[64,32]{1,0:T(8,128)S(1)} %bitcast_multiply_fusion.4), channel_id=1, source_target_pairs={{8,0},{10,2},{12,4},{14,6},{16,8},{18,10},{20,12},{22,14},{24,16},... | collective-permute-start | bytes 24584 | tf_op jit(solution)/shard_map/ppermute | solution.py:12
  90.5 56.2 %copy-start.2 = (f32[64,640]{1,0:T(8,128)}, f32[64,640]{1,0:T(8,128)S(1)}, u32[]{:S(2)}) copy-start(f32[64,640]{1,0:T(8,128)S(1)} %fusion.15) | copy-start | bytes 491524
  93.4 10.2 %collective-permute-start.11 = (f32[64,32]{1,0:T(8,128)S(1)}, f32[64,32]{1,0:T(8,128)S(1)}, u32[]{:S(2)}, u32[]{:S(2)}) collective-permute-start(f32[64,32]{1,0:T(8,128)S(1)} %bitcast_multiply_fusion), channel_id=1, source_target_pairs={{8,0},{10,2},{12,4},{14,6},{16,8},{18,10},{20,12},{22,14},{24,16},... | collective-permute-start | bytes 24584 | tf_op jit(solution)/shard_map/ppermute | solution.py:12
  94.7 8.9 %collective-permute-start.10 = (f32[64,32]{1,0:T(8,128)S(1)}, f32[64,32]{1,0:T(8,128)S(1)}, u32[]{:S(2)}, u32[]{:S(2)}) collective-permute-start(f32[64,32]{1,0:T(8,128)S(1)} %bitcast_multiply_fusion.1), channel_id=1, source_target_pairs={{0,8},{2,10},{4,12},{6,14},{8,16},{10,18},{12,20},{14,22},{16,24},... | collective-permute-start | bytes 24584 | tf_op jit(solution)/shard_map/ppermute | solution.py:12
  99.3 4.4 %collective-permute-start.9 = (f32[64,32]{1,0:T(8,128)S(1)}, f32[64,32]{1,0:T(8,128)S(1)}, u32[]{:S(2)}, u32[]{:S(2)}) collective-permute-start(f32[64,32]{1,0:T(8,128)S(1)} %bitcast_multiply_fusion.2), channel_id=1, source_target_pairs={{2,0},{4,2},{6,4},{8,6},{10,8},{12,10},{14,12},{16,14},{18,16},{20... | collective-permute-start | bytes 24584 | tf_op jit(solution)/shard_map/ppermute | solution.py:12
  100.6 3.9 %collective-permute-start.8 = (f32[64,32]{1,0:T(8,128)S(1)}, f32[64,32]{1,0:T(8,128)S(1)}, u32[]{:S(2)}, u32[]{:S(2)}) collective-permute-start(f32[64,32]{1,0:T(8,128)S(1)} %bitcast_multiply_fusion.3), channel_id=1, source_target_pairs={{0,2},{2,4},{4,6},{6,8},{8,10},{10,12},{12,14},{14,16},{16,18},{18... | collective-permute-start | bytes 24584 | tf_op jit(solution)/shard_map/ppermute | solution.py:12
where the time goes:
time: 147 us
  blocking collectives  76.4 us (52%)
  starting transfers between devices  28 us (19%)
  matrix products  17.2 us (12%)
  local copies, waits for them, and re-layouts  11.3 us (8%)
  waiting for transfers between devices  9.79 us (7%)
  other arithmetic  2.98 us (2%)
    all_gather x2, blocking collectives, precondition(): lax.all_gather(mode_coeffs.reshape(1, mode_count * rhs_width), 'sub', axi...  39.4 us
    ppermute x12, starting transfers between devices, passed_along(): return lax.ppermute(block, axis, route)  28 us
    all_gather x3, blocking collectives, extend_apply(): segment = lax.all_gather(own_and_halo, 'col', axis=1, tiled=True)  21.3 us
    psum x2, blocking collectives, precondition(): coarse_vals = lax.psum(partial_sum, 'col')  15.7 us
    dot_general x5, matrix products, extend_apply(): jnp.dot(segment, matrix, precision=HIGH)  15.4 us
    ppermute x12, waiting for transfers between devices, passed_along(): return lax.ppermute(block, axis, route)  9.79 us
    gather x24, local copies, waits for them, and re-layouts, extend_apply(): jnp.take(field, send_rows[number], axis=1) * live_slots[number][None, :]  7.86 us
  transfers between devices with their start and end apart: 12, of which 4 were waited for; matrix products, arithmetic and copies ran while one was open for 1% of the time, Pallas kernels for 0%

commit v1 on v0

v1 whole, which is shorter than its diff:
```python
import functools

import jax
import jax.numpy as jnp
from jax import lax
from jax.experimental import pallas as pl
from jax.experimental.pallas import tpu as pltpu
from jax.sharding import PartitionSpec as P

MESH = pl.DeviceIdType.MESH
F32 = jnp.float32
BF16 = jnp.bfloat16


def split(x):
    hi = x.astype(BF16)
    return hi, (x - hi.astype(F32)).astype(BF16)


def mm(x, w_hi, w_lo, dims=(((1,), (0,)), ((), ()))):
    x_hi, x_lo = split(x)
    rows = x.shape[0]
    both = lax.dot_general(
        jnp.concatenate([x_hi, x_lo], axis=0), w_hi, dims, preferred_element_type=F32
    )
    low = lax.dot_general(x_hi, w_lo, dims, preferred_element_type=F32)
    return both[:rows] + (both[rows:] + low)


def kernel(
    nsub, ncol,
    rhs_hbm, op_hbm, inv_hbm, basis_hbm, cinv_hbm, index_ref, count_ref,
    sol_ref, res_ref,
    inv_f, op_f, basis_f, cinv_f,
    inv_h, inv_l, op_h, op_l, basis_h, basis_l, cinv_h, cinv_l, sel,
    xbuf, hbuf, pack, coeff, kept, coarse, mix,
    in_sem, halo_s, halo_r, field_s, field_r, kept_s, kept_r, mix_s, mix_r, coarse_s, coarse_r,
):
    s = lax.axis_index("sub")
    c = lax.axis_index("col")
    nrhs, own = xbuf.shape[2], xbuf.shape[3]
    slots = index_ref.shape[3]
    nb = index_ref.shape[2]
    halo = nb * slots
    ch = own + halo
    modes = basis_f.shape[1]
    mq = modes // ncol
    stride = nsub // 4
    offsets = (1, -1, stride, -stride)

    loads = []
    for number, (src, dst) in enumerate((
        (rhs_hbm, xbuf.at[0, c]),
        (basis_hbm.at[0], basis_f),
        (inv_hbm.at[0], inv_f),
        (cinv_hbm, cinv_f),
        (op_hbm.at[0], op_f),
    )):
        load = pltpu.make_async_copy(src, dst, in_sem.at[number])
        load.start()
        loads.append(load)

    hbuf[...] = jnp.zeros_like(hbuf)

    barrier = pltpu.get_barrier_semaphore()

    def greet(k, carry):
        pl.semaphore_signal(
            barrier, inc=1, device_id=(lax.rem(s + k, nsub), c), device_id_type=MESH
        )
        return carry

    lax.fori_loop(1, nsub, greet, 0)
    expected = nsub - 1 + ncol - 1
    for dc in range(1, ncol):
        other = lax.rem(c + dc, ncol)
        pl.semaphore_signal(barrier, inc=1, device_id=(s, other), device_id_type=MESH)
        for d in offsets:
            t = s + d

            @pl.when(jnp.logical_and(t >= 0, t < nsub))
            def _():
                pl.semaphore_signal(barrier, inc=1, device_id=(t, other), device_id_type=MESH)

            expected = expected + jnp.where(jnp.logical_and(t >= 0, t < nsub), 1, 0)

    slot = lax.broadcasted_iota(jnp.int32, (1, slots), 1)
    row = jnp.concatenate(
        [
            jnp.where(slot < count_ref[0, 0, n], index_ref[0, 0, n : n + 1, :], -1)
            for n in range(nb)
        ],
        axis=1,
    )
    place = lax.broadcasted_iota(jnp.int32, (own, halo), 0)
    sel[...] = jnp.where(place == row, 1.0, 0.0).astype(BF16)

    def pack_rows(rnd, x):
        x_hi, x_lo = split(x)
        both = jnp.dot(
            jnp.concatenate([x_hi, x_lo], axis=0), sel[...], preferred_element_type=F32
        )
        pack[rnd] = (both[:nrhs] + both[nrhs:]).T

    def halo_copy(rnd, n, dc):
        rows = pl.ds(n * slots, slots)
        return pltpu.make_async_remote_copy(
            src_ref=pack.at[rnd, rows],
            dst_ref=hbuf.at[rnd, c, rows],
            send_sem=halo_s.at[rnd, n, dc],
            recv_sem=halo_r.at[rnd, n, c],
            device_id=(s + offsets[n], lax.rem(c + dc, ncol)),
            device_id_type=MESH,
        )

    def halo_each(rnd, act):
        for n in range(nb):
            t = s + offsets[n]

            @pl.when(jnp.logical_and(t >= 0, t < nsub))
            def _():
                for dc in range(ncol):
                    act(halo_copy(rnd, n, dc))

    def halo_wait(rnd, dc):
        source = lax.rem(c + ncol - dc, ncol)
        for n in range(nb):
            t = s - offsets[n]
            rows = pl.ds(n * slots, slots)

            @pl.when(jnp.logical_and(t >= 0, t < nsub))
            def _():
                pltpu.make_async_remote_copy(
                    src_ref=pack.at[rnd, rows],
                    dst_ref=hbuf.at[rnd, source, rows],
                    send_sem=halo_s.at[rnd, n, dc],
                    recv_sem=halo_r.at[rnd, n, source],
                    device_id=(t, source),
                    device_id_type=MESH,
                ).wait_recv()

    def peer_copy(src, buf, sems_s, sems_r, dc, arriving):
        index = lax.rem(c + ncol - dc, ncol) if arriving else c
        return pltpu.make_async_remote_copy(
            src_ref=src,
            dst_ref=buf.at[index],
            send_sem=sems_s.at[dc],
            recv_sem=sems_r.at[index],
            device_id=(s, lax.rem(c + dc, ncol)),
            device_id_type=MESH,
        )

    def field_copy(rnd, dc, arriving=False):
        return peer_copy(
            xbuf.at[rnd, c], xbuf.at[rnd], field_s.at[rnd], field_r.at[rnd], dc, arriving
        )

    def coarse_copy(rnd, dc, arriving=False):
        return peer_copy(
            coarse.at[rnd, c], coarse.at[rnd], coarse_s.at[rnd], coarse_r.at[rnd], dc, arriving
        )

    def mix_copy(dc, arriving=False):
        target = pl.multiple_of(lax.rem(c + dc, ncol) * mq, mq)
        return peer_copy(
            coeff.at[1, pl.ds(target, mq)], mix, mix_s, mix_r, dc, arriving
        )

    def kept_copy(rnd, k, arriving=False):
        index = lax.rem(s + nsub - k, nsub) if arriving else s
        return pltpu.make_async_remote_copy(
            src_ref=kept.at[rnd, s],
            dst_ref=kept.at[rnd, index],
            send_sem=kept_s.at[rnd, k],
            recv_sem=kept_r.at[rnd, index],
            device_id=(lax.rem(s + k, nsub), c),
            device_id_type=MESH,
        )

    def kept_all(rnd, act):
        def step(k, carry):
            act(k)
            return carry

        lax.fori_loop(1, nsub, step, 0)

    def split_rows(src, hi, lo, rows):
        def step(i, carry):
            at = pl.ds(pl.multiple_of(i * rows, rows), rows)
            hi[at, :], lo[at, :] = split(src[at, :])
            return carry

        lax.fori_loop(0, src.shape[0] // rows, step, 0)

    def block_rows(b):
        return pl.ds(pl.multiple_of(b * ch, 128), own)

    def halo_rows(b):
        return pl.ds(pl.multiple_of(b * ch + own, 128), halo)

    def ext_block(rnd, b):
        return jnp.concatenate([xbuf[rnd, b], hbuf[rnd, b].T], axis=1)

    def all_rows(b):
        return pl.ds(pl.multiple_of(b * ch, 128), ch)

    def coarse_sum(rnd):
        mine = pl.ds(pl.multiple_of(c * mq, mq), mq)
        kept_all(rnd, lambda k: kept_copy(rnd, k).start())
        return mine

    def coarse_solve(rnd):
        kept_all(rnd, lambda k: kept_copy(rnd, k, True).wait_recv())
        k_hi, k_lo = split(kept[rnd].reshape(nsub * mq, nrhs))
        part = jnp.dot(cinv_h[...], k_hi, preferred_element_type=F32)
        part += jnp.dot(cinv_l[...], k_hi, preferred_element_type=F32)
        part += jnp.dot(cinv_h[...], k_lo, preferred_element_type=F32)
        coarse[rnd, c] = part
        for dc in range(1, ncol):
            coarse_copy(rnd, dc).start()

    def coarse_values(rnd):
        for dc in range(1, ncol):
            coarse_copy(rnd, dc, True).wait_recv()
        return jnp.sum(coarse[rnd], axis=0).T

    def coarse_part(values, b):
        rows = block_rows(b)
        return mm(values, basis_h[rows, :], basis_l[rows, :], (((1,), (1,)), ((), ())))

    loads[0].wait()
    pack_rows(0, xbuf[0, c])
    pl.semaphore_wait(barrier, expected)
    halo_each(0, lambda copy: copy.start())
    for dc in range(1, ncol):
        field_copy(0, dc).start()
    loads[1].wait()
    split_rows(basis_f, basis_h, basis_l, 128)
    loads[2].wait()
    split_rows(inv_f, inv_h, inv_l, 128)
    loads[3].wait()
    cinv_h[...], cinv_l[...] = split(cinv_f[...])
    for dc in range(ncol):
        halo_wait(0, dc)
    for dc in range(1, ncol):
        field_copy(0, dc, True).wait_recv()

    mine = pl.ds(pl.multiple_of(c * mq, mq), mq)
    amount = jnp.zeros((nrhs, modes), F32)
    for b in range(ncol):
        rows = all_rows(b)
        amount += mm(ext_block(0, b), basis_h[rows, :], basis_l[rows, :])
    coeff[0] = amount.T
    kept[0, s] = coeff[0, mine, :]
    kept_all(0, lambda k: kept_copy(0, k).start())

    local = jnp.zeros((nrhs, own), F32)
    for b in range(ncol):
        rows = all_rows(b)
        local += mm(ext_block(0, b), inv_h[rows, :], inv_l[rows, :])
    xbuf[1, c] = local
    for dc in range(1, ncol):
        field_copy(1, dc).start()
    loads[4].wait()
    split_rows(op_f, op_h, op_l, 128)

    coarse_solve(0)
    values = coarse_values(0)
    sol_ref[...] = xbuf[1, c] + coarse_part(values, c)
    pack_rows(1, sol_ref[...])
    halo_each(1, lambda copy: copy.start())

    for dc in range(1, ncol):
        field_copy(1, dc, True).wait_recv()
    applied = jnp.zeros((nrhs, own), F32)
    for b in range(ncol):
        rows = block_rows(b)
        applied += mm(
            xbuf[1, b] + coarse_part(values, b), op_h[rows, :], op_l[rows, :]
        )
    for dc in range(ncol):
        halo_wait(1, dc)
    for b in range(ncol):
        rows = halo_rows(b)
        applied += mm(hbuf[1, b].T, op_h[rows, :], op_l[rows, :])
    residual = xbuf[0, c] - applied
    res_ref[...] = residual
    xbuf[2, c] = residual
    pack_rows(2, residual)
    halo_each(2, lambda copy: copy.start())

    rows = block_rows(c)
    amount = mm(xbuf[2, c], basis_h[rows, :], basis_l[rows, :])
    halo_wait(2, 0)
    rows = halo_rows(c)
    amount += mm(hbuf[2, c].T, basis_h[rows, :], basis_l[rows, :])
    coeff[1] = amount.T
    for dc in range(1, ncol):
        mix_copy(dc).start()
    for dc in range(1, ncol):
        field_copy(2, dc).start()
    total = coeff[1, mine, :]
    for dc in range(1, ncol):
        mix_copy(dc, True).wait_recv()
        total += mix[lax.rem(c + ncol - dc, ncol)]
    kept[1, s] = total
    kept_all(1, lambda k: kept_copy(1, k).start())

    rows = all_rows(c)
    sol_ref[...] += mm(ext_block(2, c), inv_h[rows, :], inv_l[rows, :])
    for dc in range(1, ncol):
        b = lax.rem(c + ncol - dc, ncol)
        halo_wait(2, dc)
        field_copy(2, dc, True).wait_recv()
        rows = all_rows(b)
        sol_ref[...] += mm(ext_block(2, b), inv_h[rows, :], inv_l[rows, :])
    coarse_solve(1)
    sol_ref[...] += coarse_part(coarse_values(1), c)

    for rnd in range(3):
        halo_each(rnd, lambda copy: copy.wait_send())
        for dc in range(1, ncol):
            field_copy(rnd, dc).wait_send()
    for rnd in range(2):
        kept_all(rnd, lambda k: kept_copy(rnd, k).wait_send())
        for dc in range(1, ncol):
            coarse_copy(rnd, dc).wait_send()
    for dc in range(1, ncol):
        mix_copy(dc).wait_send()


def body(
    nsub, ncol,
    right_sides, operator, local_inverse, coarse_basis, coarse_inverse, send_index, halo_count,
):
    nrhs, own = right_sides.shape
    _, ext, modes = coarse_basis.shape
    nb, slots = send_index.shape[2:]
    halo = nb * slots
    mq = modes // ncol
    kept_rows = coarse_inverse.shape[1]
    dma = pltpu.SemaphoreType.DMA
    any_spec = pl.BlockSpec(memory_space=pl.ANY)
    vmem = pl.BlockSpec(memory_space=pltpu.VMEM)
    out = jax.ShapeDtypeStruct((nrhs, own), F32)
    return pl.pallas_call(
        functools.partial(kernel, nsub, ncol),
        out_shape=(out, out),
        in_specs=[any_spec] * 5 + [vmem, pl.BlockSpec(memory_space=pltpu.SMEM)],
        out_specs=(vmem, vmem),
        scratch_shapes=[
            pltpu.VMEM((ext, own), F32),
            pltpu.VMEM((ext, own), F32),
            pltpu.VMEM((ext, modes), F32),
            pltpu.VMEM((modes, kept_rows), F32),
            pltpu.VMEM((ext, own), BF16),
            pltpu.VMEM((ext, own), BF16),
            pltpu.VMEM((ext, own), BF16),
            pltpu.VMEM((ext, own), BF16),
            pltpu.VMEM((ext, modes), BF16),
            pltpu.VMEM((ext, modes), BF16),
            pltpu.VMEM((modes, kept_rows), BF16),
            pltpu.VMEM((modes, kept_rows), BF16),
            pltpu.VMEM((own, halo), BF16),
            pltpu.VMEM((3, ncol, nrhs, own), F32),
            pltpu.VMEM((3, ncol, halo, nrhs), F32),
            pltpu.VMEM((3, halo, nrhs), F32),
            pltpu.VMEM((2, modes, nrhs), F32),
            pltpu.VMEM((2, nsub, mq, nrhs), F32),
            pltpu.VMEM((2, ncol, modes, nrhs), F32),
            pltpu.VMEM((ncol, mq, nrhs), F32),
            dma((5,)),
            dma((3, nb, ncol)),
            dma((3, nb, ncol)),
            dma((3, ncol)),
            dma((3, ncol)),
            dma((2, nsub)),
            dma((2, nsub)),
            dma((ncol,)),
            dma((ncol,)),
            dma((2, ncol)),
            dma((2, ncol)),
        ],
        compiler_params=pltpu.CompilerParams(
            collective_id=0, has_side_effects=True, vmem_limit_bytes=48 * 1024 * 1024
        ),
    )(right_sides, operator, local_inverse, coarse_basis, coarse_inverse, send_index, halo_count)


def solution(mesh):
    placed = (
        P(None, ("sub", "col")),
        P("sub", None, "col"),
        P("sub", None, "col"),
        P("sub", None, None),
        P("sub", "col"),
        P("sub", "col", None, None),
        P("sub", "col", None),
    )
    return jax.shard_map(
        functools.partial(body, mesh.shape["sub"], mesh.shape["col"]),
        mesh=mesh,
        in_specs=placed,
        out_specs=(P(None, ("sub", "col")), P(None, ("sub", "col"))),
        check_vma=False,
    )
```

time: 147 us -> 54.6 us (0.37)
  blocking collectives: 76.4 us -> 0 us
  Pallas kernels: 0 us -> 45.8 us
  starting transfers between devices: 28 us -> 0 us
  matrix products: 17.2 us -> 0 us
  waiting for transfers between devices: 9.79 us -> 0 us
  local copies, waits for them, and re-layouts: 11.3 us -> 7.86 us
  other arithmetic: 2.98 us -> 0 us
    all_gather x5 -> x0, blocking collectives: 60.7 us -> none  [the longest x2 39.4 us: precondition(): lax.all_gather(mode_coeffs.reshape(1, mode_count * rhs_width), 'sub', axi...]
    pallas_call x0 -> x1, Pallas kernels: none -> 45.8 us  [body(): pl.pallas_call(functools.partial(kernel, nsub, ncol), out_shape=(out, out...]
    ppermute x12 -> x0, starting transfers between devices: 28 us -> none  [passed_along(): return lax.ppermute(block, axis, route)]
    dot_general x9 -> x0, matrix products: 17.2 us -> none  [the longest x5 15.4 us: extend_apply(): jnp.dot(segment, matrix, precision=HIGH)]
    psum x2 -> x0, blocking collectives: 15.7 us -> none  [precondition(): coarse_vals = lax.psum(partial_sum, 'col')]
    ppermute x12 -> x0, waiting for transfers between devices: 9.79 us -> none  [passed_along(): return lax.ppermute(block, axis, route)]
    gather x24 -> x0, local copies, waits for them, and re-layouts: 7.86 us -> none  [extend_apply(): jnp.take(field, send_rows[number], axis=1) * live_slots[number][None, :]]
    unnamed x11 -> x13, local copies, waits for them, and re-layouts: 1.3 us -> 7.86 us
  transfers between devices with their start and end apart: 12 -> 0, of which waited for: 4 -> 0; matrix products, arithmetic and copies ran while one was open for 1% -> 0% of each run, Pallas kernels for 0% -> 0%
where the time goes in v1:
time: 54.6 us; the launch traced here: 54.3 us
  Pallas kernels  45.8 us (84%)
  local copies, waits for them, and re-layouts  7.86 us (14%)
  between operations  0.66 us (1%)
    pallas_call x1, Pallas kernels, body(): pl.pallas_call(functools.partial(kernel, nsub, ncol), out_shape=(out, out...  45.8 us
    unnamed x13, local copies, waits for them, and re-layouts  7.86 us

profile of v1, /device:TPU:0, one launch (start us, length us, event | category | flops | bytes accessed | tf_op | source)
XLA Modules:
  0.0 54.3 jit_solution(10666177852080788316)
XLA Ops:
  0.6 1.3 %copy.9.basis_hbm = f32[1,1536,64]{2,1,0:T(8,128)S(1)} copy(f32[1,1536,64]{1,2,0:T(8,128)} %param.10) | data formatting | bytes 786432 | tf_op args[3]
  1.9 0.0 copy-start
  1.9 2.1 %copy-done = f32[1,1536,640]{2,1,0:T(8,128)S(1)} copy-done((f32[1,1536,640]{2,1,0:T(8,128)S(1)}, f32[1,1536,640]{2,1,0:T(8,128)}, u32[]{:S(2)}) %copy-start) | copy-done | bytes 3932184
  4.0 0.0 copy-start.1
  4.0 0.9 %copy-done.1 = f32[64,640]{1,0:T(8,128)S(1)} copy-done((f32[64,640]{1,0:T(8,128)S(1)}, f32[64,640]{1,0:T(8,128)}, u32[]{:S(2)}) %copy-start.1) | copy-done | bytes 163864
  4.9 0.0 copy-start.2
  4.9 0.9 %copy-done.2 = f32[64,512]{1,0:T(8,128)S(1)} copy-done((f32[64,512]{1,0:T(8,128)S(1)}, f32[64,512]{1,0:T(8,128)}, u32[]{:S(2)}) %copy-start.2) | copy-done | bytes 131096
  5.8 0.0 copy-start.3
  5.8 0.7 %copy-done.3 = s32[1,1,4,32]{3,2,1,0:T(4,128)S(1)} copy-done((s32[1,1,4,32]{3,2,1,0:T(4,128)S(1)}, s32[1,1,4,32]{3,2,1,0:T(4,128)}, u32[]{:S(2)}) %copy-start.3) | copy-done | bytes 536
  6.5 0.0 copy-start.4
  6.5 0.7 %copy-done.4 = s32[1,1,4]{2,1,0:T(1,128)S(1)} copy-done((s32[1,1,4]{2,1,0:T(1,128)S(1)}, s32[1,1,4]{2,1,0:T(1,128)}, u32[]{:S(2)}) %copy-start.4) | copy-done | bytes 40
  7.2 45.8 %shard_map.86 = (f32[64,640]{1,0:T(8,128)S(1)}, f32[64,640]{1,0:T(8,128)S(1)}) custom-call(f32[64,640]{1,0:T(8,128)S(1)} %copy-done.1, f32[1,1536,640]{2,1,0:T(8,128)S(1)} %copy-done, f32[1,1536,640]{2,1,0:T(8,128)} %inv_hbm.1, f32[1,1536,64]{2,1,0:T(8,128)S(1)} %copy.9.basis_hbm, f32[64,512]{1,0:T(8,128)S(1)} %copy-done.2, s32[1,1,4,32]{3,2,1,0:T(4,128)S(1)} %copy-done.3, ...), custom_call_target="tpu_custom_call" | custom-call | tf_op jit(solution)/shard_map/pallas_call | solution.py:346
  52.9 0.7 %copy.12 = f32[64,640]{1,0:T(8,128)} copy(f32[64,640]{1,0:T(8,128)S(1)} %get-tuple-element.4) | data formatting | bytes 327680
  53.6 0.7 %copy.13 = f32[64,640]{1,0:T(8,128)} copy(f32[64,640]{1,0:T(8,128)S(1)} %get-tuple-element.5) | data formatting | bytes 327680
Async XLA Ops:
  1.9 2.1 %copy-start = (f32[1,1536,640]{2,1,0:T(8,128)S(1)}, f32[1,1536,640]{2,1,0:T(8,128)}, u32[]{:S(2)}) copy-start(f32[1,1536,640]{2,1,0:T(8,128)} %op_hbm.1) | copy-start | bytes 11796484
  4.0 0.9 %copy-start.1 = (f32[64,640]{1,0:T(8,128)S(1)}, f32[64,640]{1,0:T(8,128)}, u32[]{:S(2)}) copy-start(f32[64,640]{1,0:T(8,128)} %rhs_hbm.1) | copy-start | bytes 491524
  4.9 0.9 %copy-start.2 = (f32[64,512]{1,0:T(8,128)S(1)}, f32[64,512]{1,0:T(8,128)}, u32[]{:S(2)}) copy-start(f32[64,512]{1,0:T(8,128)} %cinv_hbm.1) | copy-start | bytes 393220
  5.8 0.7 %copy-start.3 = (s32[1,1,4,32]{3,2,1,0:T(4,128)S(1)}, s32[1,1,4,32]{3,2,1,0:T(4,128)}, u32[]{:S(2)}) copy-start(s32[1,1,4,32]{3,2,1,0:T(4,128)} %index_ref.1) | copy-start | bytes 1540
  6.5 0.7 %copy-start.4 = (s32[1,1,4]{2,1,0:T(1,128)S(1)}, s32[1,1,4]{2,1,0:T(1,128)}, u32[]{:S(2)}) copy-start(s32[1,1,4]{2,1,0:T(1,128)} %count_ref.1) | copy-start | bytes 52

commit v2 on v1

--- a/solution.py
+++ b/solution.py
@@ -7,6 +7,7 @@
 from jax.experimental.pallas import tpu as pltpu
 from jax.sharding import PartitionSpec as P
 
+TRANS = (((1,), (1,)), ((), ()))
 MESH = pl.DeviceIdType.MESH
 F32 = jnp.float32
 BF16 = jnp.bfloat16
@@ -27,11 +28,21 @@
     return both[:rows] + (both[rows:] + low)
 
 
+def fold(x):
+    half = x.shape[0] // 2
+    return jnp.concatenate([x[:half], x[half:]], axis=1)
+
+
+def unfold(x):
+    width = x.shape[-1] // 2
+    return jnp.concatenate([x[..., :width], x[..., width:]], axis=-2)
+
+
 def kernel(
     nsub, ncol,
-    rhs_hbm, op_hbm, inv_hbm, basis_hbm, cinv_hbm, index_ref, count_ref,
+    rhs_hbm, op_hbm, inv_hbm, basis_hbm, cinv_hbm, index_hbm, count_hbm,
     sol_ref, res_ref,
-    inv_f, op_f, basis_f, cinv_f,
+    index_ref, count_ref, inv_f, op_f, basis_f, cinv_f,
     inv_h, inv_l, op_h, op_l, basis_h, basis_l, cinv_h, cinv_l, sel,
     xbuf, hbuf, pack, coeff, kept, coarse, mix,
     in_sem, halo_s, halo_r, field_s, field_r, kept_s, kept_r, mix_s, mix_r, coarse_s, coarse_r,
@@ -43,13 +54,15 @@
     nb = index_ref.shape[2]
     halo = nb * slots
     ch = own + halo
-    modes = basis_f.shape[1]
+    modes = basis_f.shape[0]
     mq = modes // ncol
     stride = nsub // 4
     offsets = (1, -1, stride, -stride)
 
     loads = []
     for number, (src, dst) in enumerate((
+        (index_hbm, index_ref),
+        (count_hbm, count_ref),
         (rhs_hbm, xbuf.at[0, c]),
         (basis_hbm.at[0], basis_f),
         (inv_hbm.at[0], inv_f),
@@ -84,6 +97,8 @@
 
             expected = expected + jnp.where(jnp.logical_and(t >= 0, t < nsub), 1, 0)
 
+    loads[0].wait()
+    loads[1].wait()
     slot = lax.broadcasted_iota(jnp.int32, (1, slots), 1)
     row = jnp.concatenate(
         [
@@ -100,13 +115,14 @@
         both = jnp.dot(
             jnp.concatenate([x_hi, x_lo], axis=0), sel[...], preferred_element_type=F32
         )
-        pack[rnd] = (both[:nrhs] + both[nrhs:]).T
+        rows = (both[:nrhs] + both[nrhs:]).T
+        for n in range(nb):
+            pack[rnd, n] = fold(rows[n * slots : (n + 1) * slots])
 
     def halo_copy(rnd, n, dc):
-        rows = pl.ds(n * slots, slots)
         return pltpu.make_async_remote_copy(
-            src_ref=pack.at[rnd, rows],
-            dst_ref=hbuf.at[rnd, c, rows],
+            src_ref=pack.at[rnd, n],
+            dst_ref=hbuf.at[rnd, c, n],
             send_sem=halo_s.at[rnd, n, dc],
             recv_sem=halo_r.at[rnd, n, c],
             device_id=(s + offsets[n], lax.rem(c + dc, ncol)),
@@ -126,13 +142,12 @@
         source = lax.rem(c + ncol - dc, ncol)
         for n in range(nb):
             t = s - offsets[n]
-            rows = pl.ds(n * slots, slots)
 
             @pl.when(jnp.logical_and(t >= 0, t < nsub))
             def _():
                 pltpu.make_async_remote_copy(
-                    src_ref=pack.at[rnd, rows],
-                    dst_ref=hbuf.at[rnd, source, rows],
+                    src_ref=pack.at[rnd, n],
+                    dst_ref=hbuf.at[rnd, source, n],
                     send_sem=halo_s.at[rnd, n, dc],
                     recv_sem=halo_r.at[rnd, n, source],
                     device_id=(t, source),
@@ -161,9 +176,8 @@
         )
 
     def mix_copy(dc, arriving=False):
-        target = pl.multiple_of(lax.rem(c + dc, ncol) * mq, mq)
         return peer_copy(
-            coeff.at[1, pl.ds(target, mq)], mix, mix_s, mix_r, dc, arriving
+            coeff.at[lax.rem(c + dc, ncol)], mix, mix_s, mix_r, dc, arriving
         )
 
     def kept_copy(rnd, k, arriving=False):
@@ -199,59 +213,61 @@
         return pl.ds(pl.multiple_of(b * ch + own, 128), halo)
 
     def ext_block(rnd, b):
-        return jnp.concatenate([xbuf[rnd, b], hbuf[rnd, b].T], axis=1)
+        return jnp.concatenate([xbuf[rnd, b], halo_field(rnd, b)], axis=1)
 
     def all_rows(b):
         return pl.ds(pl.multiple_of(b * ch, 128), ch)
 
-    def coarse_sum(rnd):
-        mine = pl.ds(pl.multiple_of(c * mq, mq), mq)
-        kept_all(rnd, lambda k: kept_copy(rnd, k).start())
-        return mine
+    def halo_field(rnd, b):
+        return unfold(hbuf[rnd, b]).reshape(halo, nrhs).T
 
     def coarse_solve(rnd):
         kept_all(rnd, lambda k: kept_copy(rnd, k, True).wait_recv())
-        k_hi, k_lo = split(kept[rnd].reshape(nsub * mq, nrhs))
+        k_hi, k_lo = split(unfold(kept[rnd]).reshape(nsub * mq, nrhs))
         part = jnp.dot(cinv_h[...], k_hi, preferred_element_type=F32)
         part += jnp.dot(cinv_l[...], k_hi, preferred_element_type=F32)
         part += jnp.dot(cinv_h[...], k_lo, preferred_element_type=F32)
-        coarse[rnd, c] = part
+        coarse[rnd, c] = fold(part)
         for dc in range(1, ncol):
             coarse_copy(rnd, dc).start()
 
     def coarse_values(rnd):
         for dc in range(1, ncol):
             coarse_copy(rnd, dc, True).wait_recv()
-        return jnp.sum(coarse[rnd], axis=0).T
+        return unfold(jnp.sum(coarse[rnd], axis=0)).T
 
     def coarse_part(values, b):
         rows = block_rows(b)
-        return mm(values, basis_h[rows, :], basis_l[rows, :], (((1,), (1,)), ((), ())))
-
-    loads[0].wait()
+        return mm(values, basis_h[:, rows], basis_l[:, rows])
+
+    def set_coeff(amount):
+        rows = amount.T
+        for b in range(ncol):
+            coeff[b] = fold(rows[b * mq : (b + 1) * mq])
+
+    loads[2].wait()
     pack_rows(0, xbuf[0, c])
     pl.semaphore_wait(barrier, expected)
     halo_each(0, lambda copy: copy.start())
     for dc in range(1, ncol):
         field_copy(0, dc).start()
-    loads[1].wait()
-    split_rows(basis_f, basis_h, basis_l, 128)
-    loads[2].wait()
+    loads[3].wait()
+    basis_h[...], basis_l[...] = split(basis_f[...])
+    loads[4].wait()
     split_rows(inv_f, inv_h, inv_l, 128)
-    loads[3].wait()
+    loads[5].wait()
     cinv_h[...], cinv_l[...] = split(cinv_f[...])
     for dc in range(ncol):
         halo_wait(0, dc)
     for dc in range(1, ncol):
         field_copy(0, dc, True).wait_recv()
 
-    mine = pl.ds(pl.multiple_of(c * mq, mq), mq)
     amount = jnp.zeros((nrhs, modes), F32)
     for b in range(ncol):
         rows = all_rows(b)
-        amount += mm(ext_block(0, b), basis_h[rows, :], basis_l[rows, :])
-    coeff[0] = amount.T
-    kept[0, s] = coeff[0, mine, :]
+        amount += mm(ext_block(0, b), basis_h[:, rows], basis_l[:, rows], TRANS)
+    set_coeff(amount)
+    kept[0, s] = coeff[c]
     kept_all(0, lambda k: kept_copy(0, k).start())
 
     local = jnp.zeros((nrhs, own), F32)
@@ -261,7 +277,7 @@
     xbuf[1, c] = local
     for dc in range(1, ncol):
         field_copy(1, dc).start()
-    loads[4].wait()
+    loads[6].wait()
     split_rows(op_f, op_h, op_l, 128)
 
     coarse_solve(0)
@@ -282,7 +298,7 @@
         halo_wait(1, dc)
     for b in range(ncol):
         rows = halo_rows(b)
-        applied += mm(hbuf[1, b].T, op_h[rows, :], op_l[rows, :])
+        applied += mm(halo_field(1, b), op_h[rows, :], op_l[rows, :])
     residual = xbuf[0, c] - applied
     res_ref[...] = residual
     xbuf[2, c] = residual
@@ -290,16 +306,16 @@
     halo_each(2, lambda copy: copy.start())
 
     rows = block_rows(c)
-    amount = mm(xbuf[2, c], basis_h[rows, :], basis_l[rows, :])
+    amount = mm(xbuf[2, c], basis_h[:, rows], basis_l[:, rows], TRANS)
     halo_wait(2, 0)
     rows = halo_rows(c)
-    amount += mm(hbuf[2, c].T, basis_h[rows, :], basis_l[rows, :])
-    coeff[1] = amount.T
+    amount += mm(halo_field(2, c), basis_h[:, rows], basis_l[:, rows], TRANS)
+    set_coeff(amount)
     for dc in range(1, ncol):
         mix_copy(dc).start()
     for dc in range(1, ncol):
         field_copy(2, dc).start()
-    total = coeff[1, mine, :]
+    total = coeff[c]
     for dc in range(1, ncol):
         mix_copy(dc, True).wait_recv()
         total += mix[lax.rem(c + ncol - dc, ncol)]
@@ -340,36 +356,38 @@
     mq = modes // ncol
     kept_rows = coarse_inverse.shape[1]
     dma = pltpu.SemaphoreType.DMA
-    any_spec = pl.BlockSpec(memory_space=pl.ANY)
+    any_spec = pl.BlockSpec(memory_space=pltpu.HBM)
     vmem = pl.BlockSpec(memory_space=pltpu.VMEM)
     out = jax.ShapeDtypeStruct((nrhs, own), F32)
     return pl.pallas_call(
         functools.partial(kernel, nsub, ncol),
         out_shape=(out, out),
-        in_specs=[any_spec] * 5 + [vmem, pl.BlockSpec(memory_space=pltpu.SMEM)],
+        in_specs=[any_spec] * 7,
         out_specs=(vmem, vmem),
         scratch_shapes=[
+            pltpu.VMEM(send_index.shape, jnp.int32),
+            pltpu.SMEM(halo_count.shape, jnp.int32),
             pltpu.VMEM((ext, own), F32),
             pltpu.VMEM((ext, own), F32),
-            pltpu.VMEM((ext, modes), F32),
+            pltpu.VMEM((modes, ext), F32),
             pltpu.VMEM((modes, kept_rows), F32),
             pltpu.VMEM((ext, own), BF16),
             pltpu.VMEM((ext, own), BF16),
             pltpu.VMEM((ext, own), BF16),
             pltpu.VMEM((ext, own), BF16),
-            pltpu.VMEM((ext, modes), BF16),
-            pltpu.VMEM((ext, modes), BF16),
+            pltpu.VMEM((modes, ext), BF16),
+            pltpu.VMEM((modes, ext), BF16),
             pltpu.VMEM((modes, kept_rows), BF16),
             pltpu.VMEM((modes, kept_rows), BF16),
             pltpu.VMEM((own, halo), BF16),
             pltpu.VMEM((3, ncol, nrhs, own), F32),
-            pltpu.VMEM((3, ncol, halo, nrhs), F32),
-            pltpu.VMEM((3, halo, nrhs), F32),
-            pltpu.VMEM((2, modes, nrhs), F32),
-            pltpu.VMEM((2, nsub, mq, nrhs), F32),
-            pltpu.VMEM((2, ncol, modes, nrhs), F32),
-            pltpu.VMEM((ncol, mq, nrhs), F32),
-            dma((5,)),
+            pltpu.VMEM((3, ncol, nb, slots // 2, 2 * nrhs), F32),
+            pltpu.VMEM((3, nb, slots // 2, 2 * nrhs), F32),
+            pltpu.VMEM((ncol, mq // 2, 2 * nrhs), F32),
+            pltpu.VMEM((2, nsub, mq // 2, 2 * nrhs), F32),
+            pltpu.VMEM((2, ncol, modes // 2, 2 * nrhs), F32),
+            pltpu.VMEM((ncol, mq // 2, 2 * nrhs), F32),
+            dma((7,)),
             dma((3, nb, ncol)),
             dma((3, nb, ncol)),
             dma((3, ncol)),
@@ -382,9 +400,12 @@
             dma((2, ncol)),
         ],
         compiler_params=pltpu.CompilerParams(
-            collective_id=0, has_side_effects=True, vmem_limit_bytes=48 * 1024 * 1024
+            collective_id=0, has_side_effects=True, vmem_limit_bytes=56 * 1024 * 1024
         ),
-    )(right_sides, operator, local_inverse, coarse_basis, coarse_inverse, send_index, halo_count)
+    )(
+        right_sides, operator, local_inverse, jnp.swapaxes(coarse_basis, 1, 2),
+        coarse_inverse, send_index, halo_count,
+    )
 
 
 def solution(mesh):

time: 54.6 us -> 45.8 us (0.84)
  local copies, waits for them, and re-layouts: 7.86 us -> 3.18 us
  Pallas kernels: 45.8 us -> 41.8 us
    unnamed x13 -> x2, local copies, waits for them, and re-layouts: 7.86 us -> 3.18 us
    pallas_call x1, Pallas kernels: 45.8 us -> 41.8 us  [body(): pl.pallas_call(functools.partial(kernel, nsub, ncol), out_shape=(out, out...]
where the time goes in v2:
time: 45.8 us; the launch traced here: 45.6 us
  Pallas kernels  41.8 us (91%)
  local copies, waits for them, and re-layouts  3.18 us (7%)
  between operations  0.64 us (1%)
    pallas_call x1, Pallas kernels, body(): pl.pallas_call(functools.partial(kernel, nsub, ncol), out_shape=(out, out...  41.8 us
    unnamed x2, local copies, waits for them, and re-layouts  3.18 us

profile of v2, /device:TPU:0, one launch (start us, length us, event | category | flops | bytes accessed | tf_op | source)
XLA Modules:
  0.0 45.6 jit_solution(1617148678916967963)
XLA Ops:
  0.6 41.8 %shard_map.86 = (f32[64,640]{1,0:T(8,128)}, f32[64,640]{1,0:T(8,128)}) custom-call(f32[64,640]{1,0:T(8,128)} %rhs_hbm.1, f32[1,1536,640]{2,1,0:T(8,128)} %op_hbm.1, f32[1,1536,640]{2,1,0:T(8,128)} %inv_hbm.1, f32[1,64,1536]{2,1,0:T(8,128)} %bitcast.1, f32[64,512]{1,0:T(8,128)} %cinv_hbm.1, s32[1,1,4,32]{3,2,1,0:T(4,128)} %index_hbm.1, s32[1,1,4]{2,1,0:T(1,128)} %count_hbm.1), custom_call_target="tpu_custom_call" | custom-call | tf_op jit(solution)/shard_map/pallas_call | solution.py:362
  42.4 1.6 %copy.11 = f32[64,640]{1,0:T(8,128)} copy(f32[64,640]{1,0:T(8,128)} %get-tuple-element.4) | data formatting | bytes 327680
  44.0 1.6 %copy.12 = f32[64,640]{1,0:T(8,128)} copy(f32[64,640]{1,0:T(8,128)} %get-tuple-element.5) | data formatting | bytes 327680

commit v3 on v2

--- a/solution.py
+++ b/solution.py
@@ -44,8 +44,9 @@
     sol_ref, res_ref,
     index_ref, count_ref, inv_f, op_f, basis_f, cinv_f,
     inv_h, inv_l, op_h, op_l, basis_h, basis_l, cinv_h, cinv_l, sel,
-    xbuf, hbuf, pack, coeff, kept, coarse, mix,
+    xbuf, hbuf, pack, coeff, kept, coarse, mix, nco, near, parts, cbuf,
     in_sem, halo_s, halo_r, field_s, field_r, kept_s, kept_r, mix_s, mix_r, coarse_s, coarse_r,
+    nco_s, nco_r, near_s, near_r, part_s, part_r,
 ):
     s = lax.axis_index("sub")
     c = lax.axis_index("col")
@@ -74,6 +75,9 @@
         loads.append(load)
 
     hbuf[...] = jnp.zeros_like(hbuf)
+    nco[...] = jnp.zeros_like(nco)
+    cbuf[...] = jnp.zeros_like(cbuf)
+    near[...] = jnp.zeros_like(near)
 
     barrier = pltpu.get_barrier_semaphore()
 
@@ -118,41 +122,66 @@
         rows = (both[:nrhs] + both[nrhs:]).T
         for n in range(nb):
             pack[rnd, n] = fold(rows[n * slots : (n + 1) * slots])
-
-    def halo_copy(rnd, n, dc):
+        return rows
+
+    def in_range(t):
+        return jnp.logical_and(t >= 0, t < nsub)
+
+    def near_copy(src, buf, sems_s, sems_r, n, dc, arriving=False):
+        index = lax.rem(c + ncol - dc, ncol) if arriving else c
+        t = s - offsets[n] if arriving else s + offsets[n]
         return pltpu.make_async_remote_copy(
-            src_ref=pack.at[rnd, n],
-            dst_ref=hbuf.at[rnd, c, n],
-            send_sem=halo_s.at[rnd, n, dc],
-            recv_sem=halo_r.at[rnd, n, c],
-            device_id=(s + offsets[n], lax.rem(c + dc, ncol)),
+            src_ref=src,
+            dst_ref=buf.at[index, n],
+            send_sem=sems_s.at[n, dc],
+            recv_sem=sems_r.at[n, index],
+            device_id=(t, lax.rem(c + dc, ncol)),
             device_id_type=MESH,
         )
 
-    def halo_each(rnd, act):
+    def near_send(make, act):
         for n in range(nb):
-            t = s + offsets[n]
-
-            @pl.when(jnp.logical_and(t >= 0, t < nsub))
+
+            @pl.when(in_range(s + offsets[n]))
             def _():
                 for dc in range(ncol):
-                    act(halo_copy(rnd, n, dc))
+                    act(make(n, dc, False))
+
+    def near_wait(make, dc):
+        for n in range(nb):
+
+            @pl.when(in_range(s - offsets[n]))
+            def _():
+                make(n, dc, True).wait_recv()
+
+    def halo_copy(rnd):
+        return lambda n, dc, arriving: near_copy(
+            pack.at[rnd, n], hbuf.at[rnd], halo_s.at[rnd], halo_r.at[rnd], n, dc, arriving
+        )
+
+    def halo_each(rnd, act):
+        near_send(halo_copy(rnd), act)
 
     def halo_wait(rnd, dc):
-        source = lax.rem(c + ncol - dc, ncol)
-        for n in range(nb):
-            t = s - offsets[n]
-
-            @pl.when(jnp.logical_and(t >= 0, t < nsub))
-            def _():
-                pltpu.make_async_remote_copy(
-                    src_ref=pack.at[rnd, n],
-                    dst_ref=hbuf.at[rnd, source, n],
-                    send_sem=halo_s.at[rnd, n, dc],
-                    recv_sem=halo_r.at[rnd, n, source],
-                    device_id=(t, source),
-                    device_id_type=MESH,
-                ).wait_recv()
+        near_wait(halo_copy(rnd), dc)
+
+    def nco_copy(n, dc, arriving):
+        return near_copy(coarse.at[0, c], nco, nco_s, nco_r, n, dc, arriving)
+
+    def part_copy(n, dc, arriving):
+        return near_copy(
+            parts.at[n, lax.rem(c + dc, ncol)], cbuf, part_s, part_r, n, dc, arriving
+        )
+
+    def basis_copy(n):
+        return pltpu.make_async_remote_copy(
+            src_ref=basis_f.at[:, pl.ds(pl.multiple_of(c * ch + own, 128), halo)],
+            dst_ref=near.at[n],
+            send_sem=near_s.at[n],
+            recv_sem=near_r.at[n],
+            device_id=(s - offsets[n], c),
+            device_id_type=MESH,
+        )
 
     def peer_copy(src, buf, sems_s, sems_r, dc, arriving):
         index = lax.rem(c + ncol - dc, ncol) if arriving else c
@@ -230,6 +259,8 @@
         coarse[rnd, c] = fold(part)
         for dc in range(1, ncol):
             coarse_copy(rnd, dc).start()
+        if rnd == 0:
+            near_send(nco_copy, lambda copy: copy.start())
 
     def coarse_values(rnd):
         for dc in range(1, ncol):
@@ -252,7 +283,15 @@
     for dc in range(1, ncol):
         field_copy(0, dc).start()
     loads[3].wait()
+    for n in range(nb):
+
+        @pl.when(in_range(s - offsets[n]))
+        def _():
+            basis_copy(n).start()
+
     basis_h[...], basis_l[...] = split(basis_f[...])
+    pack_rows(3, basis_f[:, block_rows(c)])
+    halo_each(3, lambda copy: copy.start())
     loads[4].wait()
     split_rows(inv_f, inv_h, inv_l, 128)
     loads[5].wait()
@@ -275,6 +314,8 @@
         rows = all_rows(b)
         local += mm(ext_block(0, b), inv_h[rows, :], inv_l[rows, :])
     xbuf[1, c] = local
+    pack_rows(1, local)
+    halo_each(1, lambda copy: copy.start())
     for dc in range(1, ncol):
         field_copy(1, dc).start()
     loads[6].wait()
@@ -283,8 +324,6 @@
     coarse_solve(0)
     values = coarse_values(0)
     sol_ref[...] = xbuf[1, c] + coarse_part(values, c)
-    pack_rows(1, sol_ref[...])
-    halo_each(1, lambda copy: copy.start())
 
     for dc in range(1, ncol):
         field_copy(1, dc, True).wait_recv()
@@ -296,32 +335,61 @@
         )
     for dc in range(ncol):
         halo_wait(1, dc)
+        halo_wait(3, dc)
+        near_wait(nco_copy, dc)
+    added = []
+    for n in range(nb):
+        near_hi, near_lo = split(unfold(jnp.sum(nco[:, n], axis=0)))
+        picked = unfold(hbuf[3, :, n]).reshape(ncol * slots, modes)
+        added.append(mm(picked, near_hi, near_lo))
     for b in range(ncol):
         rows = halo_rows(b)
-        applied += mm(halo_field(1, b), op_h[rows, :], op_l[rows, :])
+        part = jnp.concatenate([x[b * slots : (b + 1) * slots] for x in added], axis=0)
+        applied += mm(halo_field(1, b) + part.T, op_h[rows, :], op_l[rows, :])
     residual = xbuf[0, c] - applied
     res_ref[...] = residual
     xbuf[2, c] = residual
-    pack_rows(2, residual)
+    rows = pack_rows(2, residual)
+
+    for n in range(nb):
+
+        @pl.when(in_range(s + offsets[n]))
+        def _():
+            basis_wait = pltpu.make_async_remote_copy(
+                src_ref=near.at[n],
+                dst_ref=near.at[n],
+                send_sem=near_s.at[n],
+                recv_sem=near_r.at[n],
+                device_id=(s + offsets[n], c),
+                device_id_type=MESH,
+            )
+            basis_wait.wait_recv()
+
+    for n in range(nb):
+        cut = slice(n * slots, (n + 1) * slots)
+        row_hi, row_lo = split(rows[cut])
+        share = mm(near[n][:, cut], row_hi, row_lo)
+        for b in range(ncol):
+            parts[n, b] = fold(share[b * mq : (b + 1) * mq])
+    near_send(part_copy, lambda copy: copy.start())
+    rows = block_rows(c)
+    amount = mm(residual, basis_h[:, rows], basis_l[:, rows], TRANS)
+    set_coeff(amount)
+    for dc in range(1, ncol):
+        mix_copy(dc).start()
     halo_each(2, lambda copy: copy.start())
-
-    rows = block_rows(c)
-    amount = mm(xbuf[2, c], basis_h[:, rows], basis_l[:, rows], TRANS)
-    halo_wait(2, 0)
-    rows = halo_rows(c)
-    amount += mm(halo_field(2, c), basis_h[:, rows], basis_l[:, rows], TRANS)
-    set_coeff(amount)
-    for dc in range(1, ncol):
-        mix_copy(dc).start()
     for dc in range(1, ncol):
         field_copy(2, dc).start()
     total = coeff[c]
     for dc in range(1, ncol):
         mix_copy(dc, True).wait_recv()
         total += mix[lax.rem(c + ncol - dc, ncol)]
-    kept[1, s] = total
+    for dc in range(ncol):
+        near_wait(part_copy, dc)
+    kept[1, s] = total + jnp.sum(cbuf[...], axis=(0, 1))
     kept_all(1, lambda k: kept_copy(1, k).start())
 
+    halo_wait(2, 0)
     rows = all_rows(c)
     sol_ref[...] += mm(ext_block(2, c), inv_h[rows, :], inv_l[rows, :])
     for dc in range(1, ncol):
@@ -333,8 +401,17 @@
     coarse_solve(1)
     sol_ref[...] += coarse_part(coarse_values(1), c)
 
+    for rnd in range(4):
+        halo_each(rnd, lambda copy: copy.wait_send())
+    near_send(nco_copy, lambda copy: copy.wait_send())
+    near_send(part_copy, lambda copy: copy.wait_send())
+    for n in range(nb):
+
+        @pl.when(in_range(s - offsets[n]))
+        def _():
+            basis_copy(n).wait_send()
+
     for rnd in range(3):
-        halo_each(rnd, lambda copy: copy.wait_send())
         for dc in range(1, ncol):
             field_copy(rnd, dc).wait_send()
     for rnd in range(2):
@@ -381,15 +458,19 @@
             pltpu.VMEM((modes, kept_rows), BF16),
             pltpu.VMEM((own, halo), BF16),
             pltpu.VMEM((3, ncol, nrhs, own), F32),
-            pltpu.VMEM((3, ncol, nb, slots // 2, 2 * nrhs), F32),
-            pltpu.VMEM((3, nb, slots // 2, 2 * nrhs), F32),
+            pltpu.VMEM((4, ncol, nb, slots // 2, 2 * nrhs), F32),
+            pltpu.VMEM((4, nb, slots // 2, 2 * nrhs), F32),
             pltpu.VMEM((ncol, mq // 2, 2 * nrhs), F32),
             pltpu.VMEM((2, nsub, mq // 2, 2 * nrhs), F32),
             pltpu.VMEM((2, ncol, modes // 2, 2 * nrhs), F32),
             pltpu.VMEM((ncol, mq // 2, 2 * nrhs), F32),
+            pltpu.VMEM((ncol, nb, modes // 2, 2 * nrhs), F32),
+            pltpu.VMEM((nb, modes, halo), F32),
+            pltpu.VMEM((nb, ncol, mq // 2, 2 * nrhs), F32),
+            pltpu.VMEM((ncol, nb, mq // 2, 2 * nrhs), F32),
             dma((7,)),
-            dma((3, nb, ncol)),
-            dma((3, nb, ncol)),
+            dma((4, nb, ncol)),
+            dma((4, nb, ncol)),
             dma((3, ncol)),
             dma((3, ncol)),
             dma((2, nsub)),
@@ -398,6 +479,12 @@
             dma((ncol,)),
             dma((2, ncol)),
             dma((2, ncol)),
+            dma((nb, ncol)),
+            dma((nb, ncol)),
+            dma((nb,)),
+            dma((nb,)),
+            dma((nb, ncol)),
+            dma((nb, ncol)),
         ],
         compiler_params=pltpu.CompilerParams(
             collective_id=0, has_side_effects=True, vmem_limit_bytes=56 * 1024 * 1024

time: 45.8 us -> 42 us (0.917)
  Pallas kernels: 41.8 us -> 38 us
    pallas_call x1, Pallas kernels: 41.8 us -> 38 us  [body(): pl.pallas_call(functools.partial(kernel, nsub, ncol), out_shape=(out, out...]
where the time goes in v3:
time: 42 us; the launch traced here: 41.8 us
  Pallas kernels  38 us (90%)
  local copies, waits for them, and re-layouts  3.18 us (8%)
  between operations  0.64 us (2%)
    pallas_call x1, Pallas kernels, body(): pl.pallas_call(functools.partial(kernel, nsub, ncol), out_shape=(out, out...  38 us
    unnamed x2, local copies, waits for them, and re-layouts  3.18 us

profile of v3, /device:TPU:0, one launch (start us, length us, event | category | flops | bytes accessed | tf_op | source)
XLA Modules:
  0.0 41.8 jit_solution(17631251750991967902)
XLA Ops:
  0.6 38.0 %shard_map.86 = (f32[64,640]{1,0:T(8,128)}, f32[64,640]{1,0:T(8,128)}) custom-call(f32[64,640]{1,0:T(8,128)} %rhs_hbm.1, f32[1,1536,640]{2,1,0:T(8,128)} %op_hbm.1, f32[1,1536,640]{2,1,0:T(8,128)} %inv_hbm.1, f32[1,64,1536]{2,1,0:T(8,128)} %bitcast.1, f32[64,512]{1,0:T(8,128)} %cinv_hbm.1, s32[1,1,4,32]{3,2,1,0:T(4,128)} %index_hbm.1, s32[1,1,4]{2,1,0:T(1,128)} %count_hbm.1), custom_call_target="tpu_custom_call" | custom-call | tf_op jit(solution)/shard_map/pallas_call | solution.py:439
  38.6 1.6 %copy.11 = f32[64,640]{1,0:T(8,128)} copy(f32[64,640]{1,0:T(8,128)} %get-tuple-element.4) | data formatting | bytes 327680
  40.2 1.6 %copy.12 = f32[64,640]{1,0:T(8,128)} copy(f32[64,640]{1,0:T(8,128)} %get-tuple-element.5) | data formatting | bytes 327680
